TPU v7x, 32 devices: a whole 2x2x4 slice. The times are simulated.
32 devices in a mesh: grp: 2 (over x), blk: 8 (over z, y), sum: 2 (over core).
Axes of the slice: x: 2, y: 2, z: 4, core: 2. Of those that a mesh axis runs over, the one named last changes fastest.
Arguments:
- points: bfloat16 [32768, 512], P(('grp', 'blk')), parts along dimension 0, may hold values from -6 to 6
- centers: bfloat16 [2048, 512], P(('blk', 'sum')), may hold values from -6 to 6
- coefficients: bfloat16 [2048, 256], P(('blk', 'sum')), may hold values from -60 to 60
- targets: float32 [32768, 256], P(('grp', 'blk'), 'sum'), parts along dimension 0, may hold values from -6 to 6
Outputs:
- residual: float32 [32768, 256], P(('grp', 'blk'), 'sum'), parts along dimension 0
There are 2 independent parts, one for each index of `grp`. A program takes and returns all parts, laid end to end along the dimension named above; an argument that names none is the same for every part. Nothing has to cross between parts.
All inputs are finite; a program needn't handle non-finite values.
Results may differ from a plain program's by a relative error of at most 0.0029.
Values may be sent and summed in bfloat16 or wider, within the bound.
A program may use at most 64 MiB of HBM per device.

v0:
```python
import math
import jax
import jax.numpy as jnp
from jax import lax
from jax.sharding import PartitionSpec as P


def kernel_sum(points, point_sq, sharpness, center_block, coef_block):
    products = lax.dot_general(
        points, center_block, (((1,), (1,)), ((), ())), preferred_element_type=jnp.float32
    )
    center_sq = jnp.sum(jnp.square(center_block.astype(jnp.float32)), axis=1)
    kernel = jnp.exp(-sharpness * (point_sq[:, None] + center_sq[None, :] - 2.0 * products)).astype(
        jnp.bfloat16
    )
    return jnp.dot(kernel, coef_block, preferred_element_type=jnp.float32)


def per_device(points, centers, coefficients, targets):
    features = points.shape[1]
    sharpness = 0.15 / math.sqrt(features)
    point_sq = jnp.sum(jnp.square(points.astype(jnp.float32)), axis=1)
    start_sum = jnp.zeros((points.shape[0], coefficients.shape[1]), jnp.float32)
    center_piece = lax.all_gather(centers, "blk", axis=0, tiled=True)
    coef_piece = lax.all_gather(coefficients, "blk", axis=0, tiled=True)
    piece_rows = center_piece.shape[0]
    block_rows = math.gcd(piece_rows, 256)
    block_count = piece_rows // block_rows
    center_blocks = center_piece.reshape(block_count, block_rows, features)
    coef_blocks = coef_piece.reshape(block_count, block_rows, coef_piece.shape[1])

    def step(inner_sum, blocks):
        return (inner_sum + kernel_sum(points, point_sq, sharpness, blocks[0], blocks[1]), None)

    result, _ = lax.scan(step, start_sum, (center_blocks, coef_blocks))
    predicted = lax.psum_scatter(result, "sum", scatter_dimension=1, tiled=True)
    return targets - predicted


def solution(mesh):
    return jax.shard_map(
        per_device,
        mesh=mesh,
        in_specs=(
            P(("grp", "blk"), None),
            P(("blk", "sum"), None),
            P(("blk", "sum"), None),
            P(("grp", "blk"), "sum"),
        ),
        out_specs=P(("grp", "blk"), "sum"),
        check_vma=False,
    )
```

profile of v0, /device:TPU:0, one launch (start us, length us, event | category | flops | bytes accessed | tf_op | source)
XLA Modules:
  0.0 91.5 jit_solution(9340841907587885446)
XLA Ops:
  6.5 0.0 copy-start
  6.5 0.0 all-gather.2.cloned.1.call-start
  6.5 0.7 all-gather.2.cloned.1.call-update
  7.3 0.0 reduce-scatter.2.cloned.1.call-start
  7.3 33.7 %all_gather.7 = bf16[1024,256]{1,0:T(8,128)(2,1)S(1)} all-gather(bf16[128,256]{1,0:T(8,128)(2,1)} %param.8), channel_id=1, replica_groups=mesh['grp'=2,'blk'=8,'sum'=2] {'blk'}, dimensions={0}, use_global_device_ids=true | all-gather | bytes 589824 | tf_op jit(solution)/shard_map/all_gather | solution.py:25
  41.1 2.1 %multiply_reduce_fusion.1 = f32[2048]{0:T(1024)S(1)} fusion(bf16[2048,512]{1,0:T(8,128)(2,1)} %param.6), kind=kLoop, calls=%fused_computation.19 | loop fusion | flops 3143680 | bytes 2105344 | tf_op jit(solution)/shard_map/reduce_sum | solution.py:22
  43.1 9.7 %all-gather.2.cloned.1.call-done = bf16[1024,512]{1,0:T(8,128)(2,1)} async-done(((bf16[128,512]{1,0:T(8,128)(2,1)}), bf16[1024,512]{1,0:T(8,128)(2,1)}) %all-gather.2.cloned.1.call-update) | async-done | bytes 1048592 | tf_op jit(solution)/shard_map/all_gather | solution.py:24
  52.8 0.0 copy-done
  52.8 20.6 %while.11 = (s32[]{:T(128)}, f32[2048,256]{1,0:T(8,128)}, f32[2048]{0:T(1024)S(1)}, bf16[4,256,512]{2,1,0:T(8,128)(2,1)}, bf16[2048,512]{1,0:T(8,128)(2,1)S(1)},...) while((s32[]{:T(128)}, f32[2048,256]{1,0:T(8,128)}, f32[2048]{0:T(1024)S(1)}, ...), condition=%wide.region_3.4_spmd.clone, body=%wide.region_1.3_spmd.clone.sunk | while | flops 809369344 | bytes 6958179 | solution.py:35
  52.8 1.1 %multiply_reduce_fusion.3 = f32[256]{0:T(256)S(1)} fusion(bf16[4,256,512]{2,1,0:T(8,128)(2,1)} %get-tuple-element.127, s32[]{:T(128)} %get-tuple-element.116), kind=kLoop, calls=%fused_computation.11.clone.1 | loop fusion | flops 392960 | bytes 263172 | tf_op jit(solution)/shard_map/while/body/eval_jaxpr/reduce_sum | solution.py:12
  53.9 3.5 %convolution_add_fusion.2 = f32[2048,256]{1,0:T(8,128)} fusion(f32[2048,256]{1,0:T(8,128)} %get-tuple-element.117, bf16[2048,512]{1,0:T(8,128)(2,1)S(1)} %get-tuple-element.128, f32[256]{0:T(256)S(1)} %multiply_reduce_fusion.3, f32[2048]{0:T(1024)S(1)} %get-tuple-element.126, pred[]{:T(512)S(6)} %compare.3, ...), kind=kOutput, calls=%fused_computation.5.clone.1 | convolution fusion | flops 808976384 | bytes 6694913 | tf_op jit(solution)/shard_map/while/body/eval_jaxpr/dot_general | solution.py:16
  57.4 1.1 %multiply_reduce_fusion.3 = f32[256]{0:T(256)S(1)} fusion(bf16[4,256,512]{2,1,0:T(8,128)(2,1)} %get-tuple-element.127, s32[]{:T(128)} %get-tuple-element.116), kind=kLoop, calls=%fused_computation.11.clone.1 | loop fusion | flops 392960 | bytes 263172 | tf_op jit(solution)/shard_map/while/body/eval_jaxpr/reduce_sum | solution.py:12
  58.5 4.2 %convolution_add_fusion.2 = f32[2048,256]{1,0:T(8,128)} fusion(f32[2048,256]{1,0:T(8,128)} %get-tuple-element.117, bf16[2048,512]{1,0:T(8,128)(2,1)S(1)} %get-tuple-element.128, f32[256]{0:T(256)S(1)} %multiply_reduce_fusion.3, f32[2048]{0:T(1024)S(1)} %get-tuple-element.126, pred[]{:T(512)S(6)} %compare.3, ...), kind=kOutput, calls=%fused_computation.5.clone.1 | convolution fusion | flops 808976384 | bytes 6694913 | tf_op jit(solution)/shard_map/while/body/eval_jaxpr/dot_general | solution.py:16
  62.8 1.1 %multiply_reduce_fusion.3 = f32[256]{0:T(256)S(1)} fusion(bf16[4,256,512]{2,1,0:T(8,128)(2,1)} %get-tuple-element.127, s32[]{:T(128)} %get-tuple-element.116), kind=kLoop, calls=%fused_computation.11.clone.1 | loop fusion | flops 392960 | bytes 263172 | tf_op jit(solution)/shard_map/while/body/eval_jaxpr/reduce_sum | solution.py:12
  63.9 4.2 %convolution_add_fusion.2 = f32[2048,256]{1,0:T(8,128)} fusion(f32[2048,256]{1,0:T(8,128)} %get-tuple-element.117, bf16[2048,512]{1,0:T(8,128)(2,1)S(1)} %get-tuple-element.128, f32[256]{0:T(256)S(1)} %multiply_reduce_fusion.3, f32[2048]{0:T(1024)S(1)} %get-tuple-element.126, pred[]{:T(512)S(6)} %compare.3, ...), kind=kOutput, calls=%fused_computation.5.clone.1 | convolution fusion | flops 808976384 | bytes 6694913 | tf_op jit(solution)/shard_map/while/body/eval_jaxpr/dot_general | solution.py:16
  68.1 1.1 %multiply_reduce_fusion.3 = f32[256]{0:T(256)S(1)} fusion(bf16[4,256,512]{2,1,0:T(8,128)(2,1)} %get-tuple-element.127, s32[]{:T(128)} %get-tuple-element.116), kind=kLoop, calls=%fused_computation.11.clone.1 | loop fusion | flops 392960 | bytes 263172 | tf_op jit(solution)/shard_map/while/body/eval_jaxpr/reduce_sum | solution.py:12
  69.2 4.2 %convolution_add_fusion.2 = f32[2048,256]{1,0:T(8,128)} fusion(f32[2048,256]{1,0:T(8,128)} %get-tuple-element.117, bf16[2048,512]{1,0:T(8,128)(2,1)S(1)} %get-tuple-element.128, f32[256]{0:T(256)S(1)} %multiply_reduce_fusion.3, f32[2048]{0:T(1024)S(1)} %get-tuple-element.126, pred[]{:T(512)S(6)} %compare.3, ...), kind=kOutput, calls=%fused_computation.5.clone.1 | convolution fusion | flops 808976384 | bytes 6694913 | tf_op jit(solution)/shard_map/while/body/eval_jaxpr/dot_general | solution.py:16
  73.4 0.0 copy-start.1
  73.4 0.0 reduce-scatter.2.cloned.1.call-update
  73.5 8.9 %reduce-scatter.2.cloned.1.call-done = f32[2048,128]{1,0:T(8,128)} async-done(((f32[2048,256]{1,0:T(8,128)}), f32[2048,128]{1,0:T(8,128)}) %reduce-scatter.2.cloned.1.call-update) | async-done | bytes 1048592 | tf_op jit(solution)/shard_map/reduce_scatter | solution.py:36
  82.4 0.0 copy-done.1
  82.4 2.3 %sub.6 = f32[2048,128]{1,0:T(8,128)} subtract(f32[2048,128]{1,0:T(8,128)S(1)} %copy-done.1, f32[2048,128]{1,0:T(8,128)} %reduce-scatter.2.cloned.1.call-done) | non-fusion elementwise | flops 262144 | bytes 3145728 | tf_op jit(solution)/shard_map/sub | solution.py:37
  (1 shorter events, 0.0 us)
Async XLA Ops:
  6.5 46.3 %copy-start = (bf16[2048,512]{1,0:T(8,128)(2,1)S(1)}, bf16[2048,512]{1,0:T(8,128)(2,1)}, u32[]{:S(2)}) copy-start(bf16[2048,512]{1,0:T(8,128)(2,1)} %param.6) | copy-start | bytes 6291460
  6.5 46.3 %all-gather.2.cloned.1.call-start = ((), (), s32[]{:S(2)}) async-start(), calls=%async_computation.1 | async-start | bytes 1179648 | tf_op jit(solution)/shard_map/all_gather | solution.py:24
  7.3 75.1 %reduce-scatter.2.cloned.1.call-start = ((), (), s32[]{:S(2)}) async-start(), calls=%async_computation.2 | async-start | bytes 3145728 | tf_op jit(solution)/shard_map/reduce_scatter | solution.py:36
  73.4 8.9 %copy-start.1 = (f32[2048,128]{1,0:T(8,128)S(1)}, f32[2048,128]{1,0:T(8,128)}, u32[]{:S(2)}) copy-start(f32[2048,128]{1,0:T(8,128)} %param.9) | copy-start | bytes 3145732
Sparse Core Ops, SparseCore 0:
  9.5 43.3 all-gather.1
  73.6 8.7 reduce-scatter.1
where the time goes:
time: 91.9 us; the launch traced here: 91.5 us
  blocking collectives  33.7 us (37%)
  waiting for transfers between devices  19.3 us (21%)
  matrix products  16.2 us (18%)
  between operations  13.4 us (15%)
  other arithmetic  8.69 us (9%)
    all_gather x1, blocking collectives, per_device(): coef_piece = lax.all_gather(coefficients, 'blk', axis=0, tiled=True)  33.7 us
    dot_general x4, matrix products, kernel_sum(): return jnp.dot(kernel, coef_block, preferred_element_type=jnp.float32)  16.2 us
    all_gather x1, waiting for transfers between devices, per_device(): center_piece = lax.all_gather(centers, 'blk', axis=0, tiled=True)  9.71 us
    reduce_scatter x1, waiting for transfers between devices, per_device(): predicted = lax.psum_scatter(result, 'sum', scatter_dimension=1, tiled=True)  8.9 us
    reduce_sum x4, other arithmetic, kernel_sum(): center_sq = jnp.sum(jnp.square(center_block.astype(jnp.float32)), axis=1)  4.32 us
    sub x1, other arithmetic, per_device(): return targets - predicted  2.3 us
    reduce_sum x1, other arithmetic, per_device(): point_sq = jnp.sum(jnp.square(points.astype(jnp.float32)), axis=1)  2.08 us
  transfers between devices with their start and end apart: 2, of which 2 were waited for; matrix products, arithmetic and copies ran while one was open for 2% of the time, Pallas kernels for 0%

commit v1 on v0

--- a/solution.py
+++ b/solution.py
@@ -22,7 +22,12 @@
     point_sq = jnp.sum(jnp.square(points.astype(jnp.float32)), axis=1)
     start_sum = jnp.zeros((points.shape[0], coefficients.shape[1]), jnp.float32)
     center_piece = lax.all_gather(centers, "blk", axis=0, tiled=True)
-    coef_piece = lax.all_gather(coefficients, "blk", axis=0, tiled=True)
+    ring = [coefficients]
+    for hop in range(7):
+        ring.append(lax.ppermute(ring[-1], "blk", [(dev, (dev + 1) % 8) for dev in range(8)]))
+    coef_piece = jnp.roll(
+        jnp.concatenate(ring[::-1], axis=0), (lax.axis_index("blk") + 1) * ring[0].shape[0], axis=0
+    )
     piece_rows = center_piece.shape[0]
     block_rows = math.gcd(piece_rows, 256)
     block_count = piece_rows // block_rows

time: 91.9 us -> 124 us (1.35)
  waiting for transfers between devices: 19.3 us -> 81.8 us
  blocking collectives: 33.7 us -> 0 us
  starting transfers between devices: 0.04 us -> 3.03 us
    ppermute x0 -> x7, waiting for transfers between devices: none -> 45.7 us  [per_device(): lax.ppermute(ring[-1], 'blk', [(dev, (dev + 1) % 8) for dev in range(8)])]
    all_gather x1 -> x0, blocking collectives: 33.7 us -> none  [per_device(): coef_piece = lax.all_gather(coefficients, 'blk', axis=0, tiled=True)]
    all_gather x1, waiting for transfers between devices: 9.71 us -> 27.6 us  [per_device(): center_piece = lax.all_gather(centers, 'blk', axis=0, tiled=True)]
    ppermute x0 -> x7, starting transfers between devices: none -> 2.98 us  [per_device(): lax.ppermute(ring[-1], 'blk', [(dev, (dev + 1) % 8) for dev in range(8)])]
  transfers between devices with their start and end apart: 2 -> 9, of which waited for: 2 -> 9; matrix products, arithmetic and copies ran while one was open for 2% -> 2% of each run, Pallas kernels for 0% -> 0%
where the time goes in v1:
time: 124 us
  waiting for transfers between devices  81.8 us (66%)
  matrix products  16.2 us (13%)
  between operations  13.6 us (11%)
  other arithmetic  8.69 us (7%)
  starting transfers between devices  3.03 us (2%)
    ppermute x7, waiting for transfers between devices, per_device(): lax.ppermute(ring[-1], 'blk', [(dev, (dev + 1) % 8) for dev in range(8)])  45.7 us
    all_gather x1, waiting for transfers between devices, per_device(): center_piece = lax.all_gather(centers, 'blk', axis=0, tiled=True)  27.6 us
    dot_general x4, matrix products, kernel_sum(): return jnp.dot(kernel, coef_block, preferred_element_type=jnp.float32)  16.2 us
    reduce_scatter x1, waiting for transfers between devices, per_device(): predicted = lax.psum_scatter(result, 'sum', scatter_dimension=1, tiled=True)  8.51 us
    reduce_sum x4, other arithmetic, kernel_sum(): center_sq = jnp.sum(jnp.square(center_block.astype(jnp.float32)), axis=1)  4.32 us
    ppermute x7, starting transfers between devices, per_device(): lax.ppermute(ring[-1], 'blk', [(dev, (dev + 1) % 8) for dev in range(8)])  2.98 us
  transfers between devices with their start and end apart: 9, of which 9 were waited for; matrix products, arithmetic and copies ran while one was open for 2% of the time, Pallas kernels for 0%

profile of v1, /device:TPU:0, one launch (start us, length us, event | category | flops | bytes accessed | tf_op | source)
XLA Modules:
  0.0 123.5 jit_solution(17929172667654986922)
XLA Ops:
  6.5 0.0 copy-start.2
  6.5 0.0 all-gather.2.cloned.1.call-start
  6.5 3.0 %collective-permute-start = (bf16[128,256]{1,0:T(8,128)(2,1)}, bf16[128,256]{1,0:T(8,128)(2,1)S(1)}, u32[]{:S(2)}, u32[]{:S(2)}) collective-permute-start(bf16[128,256]{1,0:T(8,128)(2,1)} %param.8), channel_id=1, source_target_pairs={{0,2},{2,4},{4,6},{6,8},{8,10},{10,12},{12,14},{14,0},{1,3},{3,5},... | collective-permute-start | bytes 196616 | tf_op jit(solution)/shard_map/ppermute | solution.py:27
  9.5 5.6 %collective-permute-done = bf16[128,256]{1,0:T(8,128)(2,1)S(1)} collective-permute-done((bf16[128,256]{1,0:T(8,128)(2,1)}, bf16[128,256]{1,0:T(8,128)(2,1)S(1)}, u32[]{:S(2)}, u32[]{:S(2)}) %collective-permute-start) | collective-permute-done | bytes 65568 | tf_op jit(solution)/shard_map/ppermute | solution.py:27
  15.1 0.0 collective-permute-start.1
  15.1 7.0 %collective-permute-done.1 = bf16[128,256]{1,0:T(8,128)(2,1)S(1)} collective-permute-done((bf16[128,256]{1,0:T(8,128)(2,1)S(1)}, bf16[128,256]{1,0:T(8,128)(2,1)S(1)}, u32[]{:S(2)}, u32[]{:S(2)}) %collective-permute-start.1) | collective-permute-done | bytes 65568 | tf_op jit(solution)/shard_map/ppermute | solution.py:27
  22.0 0.0 collective-permute-start.2
  22.0 7.0 %collective-permute-done.2 = bf16[128,256]{1,0:T(8,128)(2,1)S(1)} collective-permute-done((bf16[128,256]{1,0:T(8,128)(2,1)S(1)}, bf16[128,256]{1,0:T(8,128)(2,1)S(1)}, u32[]{:S(2)}, u32[]{:S(2)}) %collective-permute-start.2) | collective-permute-done | bytes 65568 | tf_op jit(solution)/shard_map/ppermute | solution.py:27
  29.0 0.0 collective-permute-start.3
  29.0 7.0 %collective-permute-done.3 = bf16[128,256]{1,0:T(8,128)(2,1)S(1)} collective-permute-done((bf16[128,256]{1,0:T(8,128)(2,1)S(1)}, bf16[128,256]{1,0:T(8,128)(2,1)S(1)}, u32[]{:S(2)}, u32[]{:S(2)}) %collective-permute-start.3) | collective-permute-done | bytes 65568 | tf_op jit(solution)/shard_map/ppermute | solution.py:27
  36.0 0.0 collective-permute-start.4
  36.0 7.4 %collective-permute-done.4 = bf16[128,256]{1,0:T(8,128)(2,1)S(1)} collective-permute-done((bf16[128,256]{1,0:T(8,128)(2,1)S(1)}, bf16[128,256]{1,0:T(8,128)(2,1)S(1)}, u32[]{:S(2)}, u32[]{:S(2)}) %collective-permute-start.4) | collective-permute-done | bytes 65568 | tf_op jit(solution)/shard_map/ppermute | solution.py:27
  43.4 0.0 collective-permute-start.5
  43.4 0.0 all-gather.2.cloned.1.call-update
  43.4 0.0 reduce-scatter.2.cloned.1.call-start
  43.4 6.9 %collective-permute-done.5 = bf16[128,256]{1,0:T(8,128)(2,1)S(1)} collective-permute-done((bf16[128,256]{1,0:T(8,128)(2,1)S(1)}, bf16[128,256]{1,0:T(8,128)(2,1)S(1)}, u32[]{:S(2)}, u32[]{:S(2)}) %collective-permute-start.5) | collective-permute-done | bytes 65568 | tf_op jit(solution)/shard_map/ppermute | solution.py:27
  50.3 0.0 collective-permute-start.6
  50.3 2.1 %multiply_reduce_fusion.1 = f32[2048]{0:T(1024)S(1)} fusion(bf16[2048,512]{1,0:T(8,128)(2,1)} %param.6), kind=kLoop, calls=%fused_computation.19 | loop fusion | flops 3143680 | bytes 2105344 | tf_op jit(solution)/shard_map/reduce_sum | solution.py:22
  52.4 0.0 copy-start
  52.4 5.0 %collective-permute-done.6 = bf16[128,256]{1,0:T(8,128)(2,1)S(1)} collective-permute-done((bf16[128,256]{1,0:T(8,128)(2,1)S(1)}, bf16[128,256]{1,0:T(8,128)(2,1)S(1)}, u32[]{:S(2)}, u32[]{:S(2)}) %collective-permute-start.6) | collective-permute-done | bytes 65568 | tf_op jit(solution)/shard_map/ppermute | solution.py:27
  57.5 0.0 copy-done.2
  57.7 27.6 %all-gather.2.cloned.1.call-done = bf16[1024,512]{1,0:T(8,128)(2,1)} async-done(((bf16[128,512]{1,0:T(8,128)(2,1)}), bf16[1024,512]{1,0:T(8,128)(2,1)}) %all-gather.2.cloned.1.call-update) | async-done | bytes 1048592 | tf_op jit(solution)/shard_map/all_gather | solution.py:24
  85.3 0.0 copy-done
  85.3 20.6 %while.11 = (s32[]{:T(128)}, f32[2048,256]{1,0:T(8,128)}, f32[2048]{0:T(1024)S(1)}, bf16[4,256,512]{2,1,0:T(8,128)(2,1)}, bf16[2048,512]{1,0:T(8,128)(2,1)S(1)},...) while((s32[]{:T(128)}, f32[2048,256]{1,0:T(8,128)}, f32[2048]{0:T(1024)S(1)}, ...), condition=%wide.region_3.4_spmd.clone, body=%wide.region_1.3_spmd.clone.sunk | while | flops 809369344 | bytes 6958179 | solution.py:40
  85.3 1.1 multiply_reduce_fusion.3
  86.3 3.5 %convolution_add_fusion.2 = f32[2048,256]{1,0:T(8,128)} fusion(f32[2048,256]{1,0:T(8,128)} %get-tuple-element.117, bf16[2048,512]{1,0:T(8,128)(2,1)S(1)} %get-tuple-element.128, f32[256]{0:T(256)S(1)} %multiply_reduce_fusion.3, f32[2048]{0:T(1024)S(1)} %get-tuple-element.126, pred[]{:T(512)S(6)} %compare.4, ...), kind=kOutput, calls=%fused_computation.5.clone.1 | convolution fusion | flops 808976384 | bytes 6694913 | tf_op jit(solution)/shard_map/while/body/eval_jaxpr/dot_general | solution.py:16
  89.9 1.1 multiply_reduce_fusion.3
  90.9 4.2 %convolution_add_fusion.2 = f32[2048,256]{1,0:T(8,128)} fusion(f32[2048,256]{1,0:T(8,128)} %get-tuple-element.117, bf16[2048,512]{1,0:T(8,128)(2,1)S(1)} %get-tuple-element.128, f32[256]{0:T(256)S(1)} %multiply_reduce_fusion.3, f32[2048]{0:T(1024)S(1)} %get-tuple-element.126, pred[]{:T(512)S(6)} %compare.4, ...), kind=kOutput, calls=%fused_computation.5.clone.1 | convolution fusion | flops 808976384 | bytes 6694913 | tf_op jit(solution)/shard_map/while/body/eval_jaxpr/dot_general | solution.py:16
  95.2 1.1 multiply_reduce_fusion.3
  96.3 4.2 %convolution_add_fusion.2 = f32[2048,256]{1,0:T(8,128)} fusion(f32[2048,256]{1,0:T(8,128)} %get-tuple-element.117, bf16[2048,512]{1,0:T(8,128)(2,1)S(1)} %get-tuple-element.128, f32[256]{0:T(256)S(1)} %multiply_reduce_fusion.3, f32[2048]{0:T(1024)S(1)} %get-tuple-element.126, pred[]{:T(512)S(6)} %compare.4, ...), kind=kOutput, calls=%fused_computation.5.clone.1 | convolution fusion | flops 808976384 | bytes 6694913 | tf_op jit(solution)/shard_map/while/body/eval_jaxpr/dot_general | solution.py:16
  100.5 1.1 multiply_reduce_fusion.3
  101.6 4.2 %convolution_add_fusion.2 = f32[2048,256]{1,0:T(8,128)} fusion(f32[2048,256]{1,0:T(8,128)} %get-tuple-element.117, bf16[2048,512]{1,0:T(8,128)(2,1)S(1)} %get-tuple-element.128, f32[256]{0:T(256)S(1)} %multiply_reduce_fusion.3, f32[2048]{0:T(1024)S(1)} %get-tuple-element.126, pred[]{:T(512)S(6)} %compare.4, ...), kind=kOutput, calls=%fused_computation.5.clone.1 | convolution fusion | flops 808976384 | bytes 6694913 | tf_op jit(solution)/shard_map/while/body/eval_jaxpr/dot_general | solution.py:16
  105.8 0.0 copy-start.1
  105.9 0.0 reduce-scatter.2.cloned.1.call-update
  105.9 8.5 %reduce-scatter.2.cloned.1.call-done = f32[2048,128]{1,0:T(8,128)} async-done(((f32[2048,256]{1,0:T(8,128)}), f32[2048,128]{1,0:T(8,128)}) %reduce-scatter.2.cloned.1.call-update) | async-done | bytes 1048592 | tf_op jit(solution)/shard_map/reduce_scatter | solution.py:41
  114.4 0.0 copy-done.1
  114.4 2.3 %sub.11 = f32[2048,128]{1,0:T(8,128)} subtract(f32[2048,128]{1,0:T(8,128)S(1)} %copy-done.1, f32[2048,128]{1,0:T(8,128)} %reduce-scatter.2.cloned.1.call-done) | non-fusion elementwise | flops 262144 | bytes 3145728 | tf_op jit(solution)/shard_map/sub | solution.py:42
  (18 shorter events, 0.2 us)
Async XLA Ops:
  6.5 51.0 %copy-start.2 = (bf16[128,256]{1,0:T(8,128)(2,1)S(1)}, bf16[128,256]{1,0:T(8,128)(2,1)}, u32[]{:S(2)}) copy-start(bf16[128,256]{1,0:T(8,128)(2,1)} %param.8) | copy-start | bytes 196612
  6.5 78.7 %all-gather.2.cloned.1.call-start = ((), (), s32[]{:S(2)}) async-start(), calls=%async_computation.1 | async-start | bytes 1179648 | tf_op jit(solution)/shard_map/all_gather | solution.py:24
  6.5 8.5 %collective-permute-start = (bf16[128,256]{1,0:T(8,128)(2,1)}, bf16[128,256]{1,0:T(8,128)(2,1)S(1)}, u32[]{:S(2)}, u32[]{:S(2)}) collective-permute-start(bf16[128,256]{1,0:T(8,128)(2,1)} %param.8), channel_id=1, source_target_pairs={{0,2},{2,4},{4,6},{6,8},{8,10},{10,12},{12,14},{14,0},{1,3},{3,5},... | collective-permute-start | bytes 196616 | tf_op jit(solution)/shard_map/ppermute | solution.py:27
  15.1 7.0 %collective-permute-start.1 = (bf16[128,256]{1,0:T(8,128)(2,1)S(1)}, bf16[128,256]{1,0:T(8,128)(2,1)S(1)}, u32[]{:S(2)}, u32[]{:S(2)}) collective-permute-start(bf16[128,256]{1,0:T(8,128)(2,1)S(1)} %collective-permute-done), channel_id=1, source_target_pairs={{0,2},{2,4},{4,6},{6,8},{8,10},{10,12},{12,14},{14,0},{1,3},{3,5},... | collective-permute-start | bytes 196616 | tf_op jit(solution)/shard_map/ppermute | solution.py:27
  22.0 7.0 %collective-permute-start.2 = (bf16[128,256]{1,0:T(8,128)(2,1)S(1)}, bf16[128,256]{1,0:T(8,128)(2,1)S(1)}, u32[]{:S(2)}, u32[]{:S(2)}) collective-permute-start(bf16[128,256]{1,0:T(8,128)(2,1)S(1)} %collective-permute-done.1), channel_id=1, source_target_pairs={{0,2},{2,4},{4,6},{6,8},{8,10},{10,12},{12,14},{14,0},{1,3},{3,5},... | collective-permute-start | bytes 196616 | tf_op jit(solution)/shard_map/ppermute | solution.py:27
  29.0 7.0 %collective-permute-start.3 = (bf16[128,256]{1,0:T(8,128)(2,1)S(1)}, bf16[128,256]{1,0:T(8,128)(2,1)S(1)}, u32[]{:S(2)}, u32[]{:S(2)}) collective-permute-start(bf16[128,256]{1,0:T(8,128)(2,1)S(1)} %collective-permute-done.2), channel_id=1, source_target_pairs={{0,2},{2,4},{4,6},{6,8},{8,10},{10,12},{12,14},{14,0},{1,3},{3,5},... | collective-permute-start | bytes 196616 | tf_op jit(solution)/shard_map/ppermute | solution.py:27
  36.0 7.4 %collective-permute-start.4 = (bf16[128,256]{1,0:T(8,128)(2,1)S(1)}, bf16[128,256]{1,0:T(8,128)(2,1)S(1)}, u32[]{:S(2)}, u32[]{:S(2)}) collective-permute-start(bf16[128,256]{1,0:T(8,128)(2,1)S(1)} %collective-permute-done.3), channel_id=1, source_target_pairs={{0,2},{2,4},{4,6},{6,8},{8,10},{10,12},{12,14},{14,0},{1,3},{3,5},... | collective-permute-start | bytes 196616 | tf_op jit(solution)/shard_map/ppermute | solution.py:27
  43.4 7.0 %collective-permute-start.5 = (bf16[128,256]{1,0:T(8,128)(2,1)S(1)}, bf16[128,256]{1,0:T(8,128)(2,1)S(1)}, u32[]{:S(2)}, u32[]{:S(2)}) collective-permute-start(bf16[128,256]{1,0:T(8,128)(2,1)S(1)} %collective-permute-done.4), channel_id=1, source_target_pairs={{0,2},{2,4},{4,6},{6,8},{8,10},{10,12},{12,14},{14,0},{1,3},{3,5},... | collective-permute-start | bytes 196616 | tf_op jit(solution)/shard_map/ppermute | solution.py:27
  43.4 71.0 %reduce-scatter.2.cloned.1.call-start = ((), (), s32[]{:S(2)}) async-start(), calls=%async_computation.2 | async-start | bytes 3145728 | tf_op jit(solution)/shard_map/reduce_scatter | solution.py:41
  50.3 7.1 %collective-permute-start.6 = (bf16[128,256]{1,0:T(8,128)(2,1)S(1)}, bf16[128,256]{1,0:T(8,128)(2,1)S(1)}, u32[]{:S(2)}, u32[]{:S(2)}) collective-permute-start(bf16[128,256]{1,0:T(8,128)(2,1)S(1)} %collective-permute-done.5), channel_id=1, source_target_pairs={{0,2},{2,4},{4,6},{6,8},{8,10},{10,12},{12,14},{14,0},{1,3},{3,5},... | collective-permute-start | bytes 196616 | tf_op jit(solution)/shard_map/ppermute | solution.py:27
  52.4 32.9 %copy-start = (bf16[2048,512]{1,0:T(8,128)(2,1)S(1)}, bf16[2048,512]{1,0:T(8,128)(2,1)}, u32[]{:S(2)}) copy-start(bf16[2048,512]{1,0:T(8,128)(2,1)} %param.6) | copy-start | bytes 6291460
  105.8 8.5 %copy-start.1 = (f32[2048,128]{1,0:T(8,128)S(1)}, f32[2048,128]{1,0:T(8,128)}, u32[]{:S(2)}) copy-start(f32[2048,128]{1,0:T(8,128)} %param.9) | copy-start | bytes 3145732
Sparse Core Ops, SparseCore 0:
  43.5 41.7 all-gather.1
  106.0 8.3 reduce-scatter.1
